TPU v7x, 32 devices: a whole 2x2x4 slice. The times are simulated.
32 devices in a mesh: parts: 1, store: 8 (over z, y), tensor: 4 (over x, core), sub: 1.
Axes of the slice: x: 2, y: 2, z: 4, core: 2. Of those that a mesh axis runs over, the one named last changes fastest.
Arguments:
- tokens: bfloat16 [8192, 8192], P(('parts', 'store', 'tensor')), may hold values from -6 to 6
- attention_norm_gain: float32 [8192], replicated, may hold values from 0.25 to 1.75
- key_weight: bfloat16 [8192, 1024], P(None, ('tensor', 'sub')), may hold values from -0.0625 to 0.0625
- value_weight: bfloat16 [8192, 1024], P(None, ('tensor', 'sub')), may hold values from -0.0625 to 0.0625
- adapter_down_weight: bfloat16 [24, 8192, 128], P(('parts', 'store'), ('tensor', 'sub')), may hold values from -0.0625 to 0.0625
- adapter_up_weight: bfloat16 [24, 2, 64, 1024], P(('parts', 'store'), None, None, ('tensor', 'sub')), may hold values from -0.75 to 0.75
- storage_slot_adapter: int32 [24], P('parts'), may hold values from 0 to 23, as said below
- request_adapter: int32 [48], P('parts'), may hold values from 0 to 23, as said below
- segment_blocks: int32 [8, 6], P(('parts', 'store')), may hold values from 1 to 2, 8 in all within a row
Outputs:
- keys: bfloat16 [8192, 1024], P(('parts', 'store'), ('tensor', 'sub'))
- values: bfloat16 [8192, 1024], P(('parts', 'store'), ('tensor', 'sub'))
Inputs may be any that keep to these rules, and one draw needn't show every extreme that they name: `storage_slot_adapter`: a permutation: each adapter id stands in exactly one slot; slot q is stored on store index q // 3. `request_adapter`: requests g * 6 to (g + 1) * 6 - 1 belong to store group g; request j of store group g names an adapter stored on store index (g + n / 2 + j * (n / 2 - 1)) modulo n, with n the number of store indices. `segment_blocks`: row g holds the lengths of store group g's requests in order, in blocks of 128 rows; they add up to 8.
All inputs are finite; a program needn't handle non-finite values.
Results may differ from a plain program's by a relative error of at most 0.0051.
Values may be sent and summed in bfloat16 or wider, within the bound.
A program may use at most 128 MiB of HBM per device.

v0:
```python
import jax
import jax.numpy as jnp
from jax import lax
from jax.sharding import PartitionSpec as P

HD = 128
ADAPTER_RANK = 64
BLOCK = 128


adapter_scale = 0.5
rope_base = 500000.0


def apply_rotary(pre_rot, token_positions):
    row_count = pre_rot.shape[0]
    half_width = HD // 2
    frequency = rope_base ** (-2.0 * jnp.arange(half_width, dtype=jnp.float32) / HD)
    angles = token_positions.astype(jnp.float32)[:, None] * frequency[None, :]
    cosine_part = jnp.cos(angles)[:, None, :]
    sine_part = jnp.sin(angles)[:, None, :]
    heads = pre_rot.reshape(row_count, pre_rot.shape[1] // HD, HD)
    first_half = heads[:, :, :half_width]
    second_half = heads[:, :, half_width:]
    turned = jnp.concatenate(
        [
            first_half * cosine_part - second_half * sine_part,
            second_half * cosine_part + first_half * sine_part,
        ],
        axis=2,
    )
    return turned.reshape(row_count, pre_rot.shape[1])


def find_slots(adapter_ids, storage_slot_adapter):
    slot_iota = jnp.arange(storage_slot_adapter.shape[0], dtype=jnp.int32)
    hits = adapter_ids[..., None] == storage_slot_adapter
    return jnp.sum(jnp.where(hits, slot_iota, 0), axis=-1)


def block_layout(block_count, seg_row, group_req):
    seg_end = jnp.cumsum(seg_row)
    block_iota = jnp.arange(block_count, dtype=jnp.int32)
    which_seg = jnp.sum((seg_end[None, :] <= block_iota[:, None]).astype(jnp.int32), axis=1)
    seg_iota = jnp.arange(seg_row.shape[0], dtype=jnp.int32)
    picked = seg_iota[None, :] == which_seg[:, None]
    block_adapter = jnp.sum(jnp.where(picked, group_req[None, :], 0), axis=1)
    first_block = jnp.sum(jnp.where(picked, (seg_end - seg_row)[None, :], 0), axis=1)
    return (block_adapter, block_iota - first_block)


def per_device(
    tokens,
    attention_norm_gain,
    key_weight,
    value_weight,
    adapter_down_weight,
    adapter_up_weight,
    storage_slot_adapter,
    request_adapter,
    segment_blocks,
):
    wide = tokens.astype(jnp.float32)
    factor = lax.rsqrt(jnp.mean(wide * wide, axis=1, keepdims=True) + 1e-05)
    normed = (wide * factor * attention_norm_gain[None, :]).astype(jnp.bfloat16)
    shared_width = adapter_down_weight.shape[1]
    column_width = key_weight.shape[1]
    feature_start = lax.axis_index(("tensor", "sub")) * shared_width
    piece = lax.all_gather(normed, "tensor", axis=0, tiled=True)
    keys_part = jnp.dot(piece, key_weight, preferred_element_type=jnp.float32)
    values_part = jnp.dot(piece, value_weight, preferred_element_type=jnp.float32)
    feature_cols = lax.dynamic_slice_in_dim(piece, feature_start, shared_width, 1).astype(
        jnp.float32
    )
    gathered = jnp.concatenate([keys_part, values_part, feature_cols], axis=1)
    plain_keys = gathered[:, :column_width]
    plain_values = gathered[:, column_width : 2 * column_width]
    feature_rows = gathered[:, 2 * column_width :].astype(jnp.bfloat16)
    block_count = gathered.shape[0] // BLOCK
    seg_count = segment_blocks.shape[1]
    group = lax.axis_index("store")
    group_req = lax.dynamic_slice_in_dim(request_adapter, group * seg_count, seg_count)
    block_adapter, block_offset = block_layout(block_count, segment_blocks[0], group_req)
    block_slot = find_slots(block_adapter, storage_slot_adapter)
    down_table, up_table = (
        lax.all_gather(adapter_down_weight, "store", axis=0, tiled=True),
        lax.all_gather(adapter_up_weight, "store", axis=0, tiled=True),
    )
    block_down = down_table[block_slot]
    block_up = up_table[block_slot]
    partial_sum = jnp.einsum(
        "bnd,bdk->bnk",
        feature_rows.reshape(block_count, BLOCK, shared_width),
        block_down,
        preferred_element_type=jnp.float32,
    ).reshape(block_count * BLOCK, 2 * ADAPTER_RANK)
    shrunk = lax.psum(partial_sum, ("tensor", "sub")).astype(jnp.bfloat16)
    delta = jnp.einsum(
        "bnsr,bsrc->sbnc",
        shrunk.reshape(block_count, BLOCK, 2, ADAPTER_RANK),
        block_up,
        preferred_element_type=jnp.float32,
    )
    adapter_keys = delta[0].reshape(-1, column_width)
    adapter_values = delta[1].reshape(-1, column_width)
    row_iota = jnp.arange(BLOCK, dtype=jnp.int32)
    token_positions = (block_offset[:, None] * BLOCK + row_iota[None, :]).reshape(-1)
    keys = apply_rotary(plain_keys + adapter_scale * adapter_keys, token_positions).astype(
        jnp.bfloat16
    )
    values = (plain_values + adapter_scale * adapter_values).astype(jnp.bfloat16)
    return (keys, values)


def solution(mesh):
    in_specs = (
        P(("parts", "store", "tensor"), None),
        P(),
        P(None, ("tensor", "sub")),
        P(None, ("tensor", "sub")),
        P(("parts", "store"), ("tensor", "sub"), None),
        P(("parts", "store"), None, None, ("tensor", "sub")),
        P("parts"),
        P("parts"),
        P(("parts", "store"), None),
    )
    out_specs = (P(("parts", "store"), ("tensor", "sub")), P(("parts", "store"), ("tensor", "sub")))
    return jax.shard_map(
        per_device, mesh=mesh, in_specs=in_specs, out_specs=out_specs, check_vma=False
    )
```

profile of v0, /device:TPU:0, one launch (start us, length us, event | category | flops | bytes accessed | tf_op | source)
XLA Modules:
  0.0 392.0 jit_solution(1243959181959955997)
XLA Ops:
  7.2 0.7 all-gather.8.cloned.1.call-update
  7.9 0.0 all-gather.6.cloned.1.call-start
  8.0 0.7 all-gather.6.cloned.1.call-update
  8.7 0.0 all-gather.4.cloned.1.call-start
  8.7 3.3 fusion
  12.0 0.2 copy-done.1
  12.2 3.1 fusion.2
  15.3 0.6 copy-done.5
  15.9 0.2 reduce-window.4
  16.1 0.1 dynamic_slice.7
  16.2 0.1 convert_reduce_fusion
  16.3 0.2 select_reduce_fusion
  16.5 0.2 select_reduce_fusion.1
  16.7 0.1 convert_bitcast_fusion.1
  16.8 1.7 multiply_cosine_fusion
  18.5 38.6 %all-gather.8.cloned.1.call-done = bf16[24,2,64,256]{3,2,1,0:T(8,128)(2,1)} async-done(((bf16[3,2,64,256]{3,2,1,0:T(8,128)(2,1)}), bf16[24,2,64,256]{3,2,1,0:T(8,128)(2,1)}) %all-gather.8.cloned.1.call-update) | async-done | bytes 1572880 | tf_op jit(solution)/shard_map/all_gather | solution.py:87
  57.2 2.0 gather_fusion.1
  59.2 175.5 %all-gather.6.cloned.1.call-done = bf16[24,2048,128]{2,1,0:T(8,128)(2,1)} async-done(((bf16[3,2048,128]{2,1,0:T(8,128)(2,1)}), bf16[24,2048,128]{2,1,0:T(8,128)(2,1)}) %all-gather.6.cloned.1.call-update) | async-done | bytes 12582928 | tf_op jit(solution)/shard_map/all_gather | solution.py:86
  234.6 7.8 %gather_fusion = bf16[8,2048,128]{2,1,0:T(8,128)(2,1)} fusion(bf16[24,2048,128]{2,1,0:T(8,128)(2,1)} %all-gather.6.cloned.1.call-done, s32[1024]{0:T(1024)S(1)} %pad_clamp_fusion), kind=kCustom, calls=%fused_computation | custom fusion | bytes 8388640 | tf_op jit(solution)/shard_map/gather | solution.py:89
  242.4 97.9 %all-gather.4.cloned.1.call-done = bf16[1024,8192]{1,0:T(8,128)(2,1)} async-done(((bf16[256,8192]{1,0:T(8,128)(2,1)}), bf16[1024,8192]{1,0:T(8,128)(2,1)}) %all-gather.4.cloned.1.call-update) | async-done | bytes 16777232 | tf_op jit(solution)/shard_map/all_gather | solution.py:69
  340.3 2.7 constant_dynamic-slice_fusion
  343.0 0.8 copy-done
  343.8 1.2 fusion.9
  345.0 0.2 copy.24
  345.2 16.3 %all-reduce.1 = bf16[1024,128]{0,1:T(8,128)(2,1)S(1)} all-reduce(f32[1024,128]{0,1:T(8,128)S(1)} %copy.24), channel_id=1, replica_groups=mesh['parts'=1,'store'=8,'tensor'=4,'sub'=1] {'tensor','sub'}, use_global_device_ids=true, to_apply=%region_5.6 | all-reduce | flops 131072 | bytes 786432 | tf_op jit(solution)/shard_map/psum | solution.py:97
  361.6 0.5 fusion.4
  362.1 0.1 slice_multiply_fusion
  362.3 0.3 copy.29
  362.6 9.4 %convolution_add_fusion.1 = f32[1024,256]{0,1:T(8,128)S(1)} fusion(f32[1024,256]{0,1:T(8,128)S(1)} %copy.29, bf16[1024,8192]{1,0:T(8,128)(2,1)} %all-gather.4.cloned.1.call-done, bf16[8192,256]{1,0:T(8,128)(2,1)} %param.11), kind=kOutput, calls=%fused_computation.8 | convolution fusion | flops 4295229440 | bytes 23068672 | tf_op jit(solution)/shard_map/dot_general | solution.py:70
  372.0 0.2 subtract_convert_fusion
  372.3 1.0 copy.30
  373.3 12.2 %fusion.3 = bf16[1024,256]{1,0:T(8,128)(2,1)} fusion(f32[1024,256]{1,0:T(8,128)S(1)} %bitcast.39, bf16[1024,8192]{1,0:T(8,128)(2,1)} %all-gather.4.cloned.1.call-done, bf16[8192,256]{1,0:T(8,128)(2,1)} %param.12), kind=kOutput, calls=%fused_computation.9 | convolution fusion | flops 4295491584 | bytes 22544384 | tf_op jit(solution)/shard_map/dot_general | solution.py:71
  (21 shorter events, 0.2 us)
Async XLA Ops:
  7.2 4.8 %copy-start.3 = (f32[8192]{0:T(1024)S(1)}, f32[8192]{0:T(1024)}, u32[]{:S(2)}) copy-start(f32[8192]{0:T(1024)} %param.10) | copy-start | bytes 98308
  7.2 50.0 %all-gather.8.cloned.1.call-start = ((), (), s32[]{:S(2)}) async-start(), calls=%async_computation.2 | async-start | bytes 1769472 | tf_op jit(solution)/shard_map/all_gather | solution.py:87
  7.9 226.7 %all-gather.6.cloned.1.call-start = ((), (), s32[]{:S(2)}) async-start(), calls=%async_computation.1 | async-start | bytes 14155776 | tf_op jit(solution)/shard_map/all_gather | solution.py:86
  8.7 331.7 %all-gather.4.cloned.1.call-start = ((), (), s32[]{:S(2)}) async-start(), calls=%async_computation | async-start | bytes 20971520 | tf_op jit(solution)/shard_map/all_gather | solution.py:69
  8.7 3.5 copy-start.1
  15.3 0.7 copy-start.5
  15.3 0.8 copy-start.4
  15.3 1.2 copy-start.6
  340.3 3.5 copy-start
  362.6 9.4 %copy-start.2 = (f32[1024,64]{0,1:T(8,128)S(1)}, f32[1024,64]{0,1:T(8,128)}, u32[]{:S(2)}) copy-start(f32[1024,64]{0,1:T(8,128)} %get-tuple-element.9) | copy-start | bytes 786436
Sparse Core Ops, SparseCore 0:
  10.2 46.9 all-gather.7
  59.3 175.2 all-gather.5
  236.2 104.0 all-gather.3
where the time goes:
time: 392 us
  waiting for transfers between devices  313 us (80%)
  matrix products  23.4 us (6%)
  blocking collectives  16.3 us (4%)
  local copies, waits for them, and re-layouts  15.7 us (4%)
  between operations  13.9 us (4%)
  other arithmetic  9.25 us (2%)
    all_gather x1, waiting for transfers between devices, per_device(): lax.all_gather(adapter_down_weight, 'store', axis=0, tiled=True)  175 us
    all_gather x1, waiting for transfers between devices, per_device(): piece = lax.all_gather(normed, 'tensor', axis=0, tiled=True)  97.9 us
    all_gather x1, waiting for transfers between devices, per_device(): lax.all_gather(adapter_up_weight, 'store', axis=0, tiled=True)  38.6 us
    psum x1, blocking collectives, per_device(): shrunk = lax.psum(partial_sum, ('tensor', 'sub')).astype(jnp.bfloat16)  16.3 us
    dot_general x1, matrix products, per_device(): jnp.dot(piece, value_weight, preferred_element_type=jnp.float32)  12.2 us
    dot_general x1, matrix products, per_device(): keys_part = jnp.dot(piece, key_weight, preferred_element_type=jnp.float32)  9.4 us
  transfers between devices with their start and end apart: 3, of which 3 were waited for; matrix products, arithmetic and copies ran while one was open for 5% of the time, Pallas kernels for 0%

commit v1 on v0

--- a/solution.py
+++ b/solution.py
@@ -1,6 +1,11 @@
+import functools
+
 import jax
 import jax.numpy as jnp
+import numpy as np
 from jax import lax
+from jax.experimental import pallas as pl
+from jax.experimental.pallas import tpu as pltpu
 from jax.sharding import PartitionSpec as P
 
 HD = 128
@@ -112,6 +117,327 @@
     return (keys, values)
 
 
+CHUNK = 32
+
+
+def fused_kernel(
+    n_store,
+    tok_hbm, gain, kw_hbm, vw_hbm, down_hbm, up_hbm, slots, req, seg, cos_ref, sin_ref,
+    keys_out, vals_out,
+    tok, rows, kw, vw, down, up, sdown, sup, rdown, rup, acck, accv, part, rs1, mid, rs2, sh,
+    tok_sem, w_sem, xs_sem, xr_sem, ss_sem, sr_sem, fs_sem, fr_sem,
+    ds_sem, dr_sem, us_sem, ur_sem, es_sem, er_sem,
+):
+    n_chunk = rows.shape[1]
+    shard = n_chunk * CHUNK
+    seg_count = rdown.shape[0]
+    stored = down.shape[0]
+    depth = down.shape[1]
+    n_block = part.shape[0]
+    half = n_block // 2
+    store = lax.axis_index("store")
+    t = lax.axis_index("tensor")
+    x, c = t // 2, t % 2
+    ox, oc = 1 - x, 1 - c
+    peer = {"tensor": ox * 2 + c}
+    sibling = {"tensor": x * 2 + oc}
+    offsets = [(n_store // 2 + j * (n_store // 2 - 1)) % n_store for j in range(seg_count)]
+    remote = [j for j in range(seg_count) if offsets[j] != 0]
+
+    def dst_of(j):
+        return lax.rem(store + (n_store - offsets[j]), n_store)
+
+    def src_of(j):
+        return lax.rem(store + offsets[j], n_store)
+
+    def tok_copy(k):
+        r = pl.ds(pl.multiple_of(k * CHUNK, CHUNK), CHUNK)
+        return pltpu.make_async_copy(tok_hbm.at[r], tok.at[r], tok_sem.at[k])
+
+    loads = [
+        pltpu.make_async_copy(down_hbm, down, w_sem.at[0]),
+        pltpu.make_async_copy(up_hbm, up, w_sem.at[1]),
+        pltpu.make_async_copy(kw_hbm, kw, w_sem.at[2]),
+        pltpu.make_async_copy(vw_hbm, vw, w_sem.at[3]),
+    ]
+    tok_copy(0).start()
+    loads[0].start()
+    loads[1].start()
+    for k in range(1, n_chunk):
+        tok_copy(k).start()
+    loads[2].start()
+    loads[3].start()
+
+    barrier = pltpu.get_barrier_semaphore()
+    greet = [peer, sibling]
+    for j in remote:
+        greet += [{"store": dst_of(j)}, {"store": src_of(j)}]
+    for who in greet:
+        pl.semaphore_signal(barrier, inc=1, device_id=who, device_id_type=pl.DeviceIdType.MESH)
+
+    def remote_copy(src, dst, ssem, rsem, who):
+        return pltpu.make_async_remote_copy(
+            src_ref=src, dst_ref=dst, send_sem=ssem, recv_sem=rsem,
+            device_id=who, device_id_type=pl.DeviceIdType.MESH,
+        )
+
+    def x_copy(k):
+        return remote_copy(rows.at[x, k, c], rows.at[x, k, c], xs_sem.at[k], xr_sem.at[k], peer)
+
+    def s_copy(k):
+        return remote_copy(rows.at[x, k, c], rows.at[x, k, c], ss_sem.at[k], sr_sem.at[k], sibling)
+
+    def f_copy(k):
+        return remote_copy(rows.at[ox, k, c], rows.at[ox, k, c], fs_sem.at[k], fr_sem.at[k], sibling)
+
+    def d_copy(j):
+        return remote_copy(sdown.at[j], rdown.at[j], ds_sem.at[j], dr_sem.at[j], {"store": dst_of(j)})
+
+    def u_copy(j):
+        return remote_copy(sup.at[j], rup.at[j], us_sem.at[j], ur_sem.at[j], {"store": dst_of(j)})
+
+    def normalize(k):
+        tok_copy(k).wait()
+
+        def group(i, carry):
+            r = pl.ds(pl.multiple_of(k * CHUNK + i * 16, 16), 16)
+            wide = tok[r, :].astype(jnp.float32)
+            factor = lax.rsqrt(jnp.mean(wide * wide, axis=1, keepdims=True) + 1e-05)
+            rows[x, k, c, pl.ds(pl.multiple_of(i * 16, 16), 16), :] = (
+                wide * factor * gain[...]
+            ).astype(jnp.bfloat16)
+            return carry
+
+        lax.fori_loop(0, CHUNK // 16, group, 0)
+
+    normalize(0)
+    pl.semaphore_wait(barrier, len(greet))
+    x_copy(0).start()
+    s_copy(0).start()
+
+    loads[0].wait()
+    loads[1].wait()
+    for j in range(seg_count):
+        wanted = req[dst_of(j) * seg_count + j]
+        local = jnp.int32(0)
+        for i in range(1, stored):
+            local = jnp.where(slots[store * stored + i] == wanted, jnp.int32(i), local)
+        if j in remote:
+            sdown[j] = down[local]
+            sup[j] = up[local]
+            d_copy(j).start()
+            u_copy(j).start()
+        else:
+            rdown[j] = down[local]
+            rup[j] = up[local]
+
+    normalize(1)
+    x_copy(1).start()
+    s_copy(1).start()
+
+    def prepare(k, carry):
+        normalize(k)
+        s_copy(k).start()
+        return carry
+
+    lax.fori_loop(2, n_chunk, prepare, 0)
+
+    loads[2].wait()
+    loads[3].wait()
+
+    def project(xi, k, ci, count):
+        at = pl.ds(pl.multiple_of((xi * 2 + ci) * shard + k * CHUNK, CHUNK), count * CHUNK)
+        lhs = rows[xi, pl.ds(k, count), ci].reshape(count * CHUNK, kw.shape[0])
+        acck[at, :] = jnp.dot(lhs, kw[...], preferred_element_type=jnp.float32)
+        accv[at, :] = jnp.dot(lhs, vw[...], preferred_element_type=jnp.float32)
+
+    group = 4
+
+    def local_rows(i, carry):
+        project(x, i * group, c, group)
+        return carry
+
+    lax.fori_loop(0, n_chunk // group, local_rows, 0)
+
+    def sibling_rows(i, carry):
+        def arrived(k, inner):
+            s_copy(i * group + k).wait()
+            return inner
+
+        lax.fori_loop(0, group, arrived, 0)
+        project(x, i * group, oc, group)
+        return carry
+
+    lax.fori_loop(0, n_chunk // group, sibling_rows, 0)
+
+    def far_rows(k, carry):
+        x_copy(k).wait()
+        f_copy(k).start()
+
+        @pl.when(k + 2 < n_chunk)
+        def _():
+            x_copy(k + 2).start()
+
+        f_copy(k).wait()
+        lhs = rows[ox, k].reshape(2 * CHUNK, kw.shape[0])
+        pk = jnp.dot(lhs, kw[...], preferred_element_type=jnp.float32)
+        pv = jnp.dot(lhs, vw[...], preferred_element_type=jnp.float32)
+        for ci in range(2):
+            at = pl.ds(pl.multiple_of((ox * 2 + ci) * shard + k * CHUNK, CHUNK), CHUNK)
+            acck[at, :] = pk[ci * CHUNK : (ci + 1) * CHUNK]
+            accv[at, :] = pv[ci * CHUNK : (ci + 1) * CHUNK]
+        return carry
+
+    lax.fori_loop(0, n_chunk, far_rows, 0)
+
+    for j in remote:
+        d_copy(j).wait()
+        u_copy(j).wait()
+
+    def layout(b):
+        end, which, first = jnp.int32(0), jnp.int32(0), jnp.int32(0)
+        for j in range(seg_count):
+            end = end + seg[0, j]
+            past = end <= b
+            which = which + jnp.where(past, jnp.int32(1), jnp.int32(0))
+            first = jnp.where(past, end, first)
+        return jnp.minimum(which, seg_count - 1), jnp.minimum(b - first, cos_ref.shape[0] - 1)
+
+    per_block = BLOCK // CHUNK
+    per_shard = shard // BLOCK
+
+    def shrink(b, carry):
+        which, _ = layout(b)
+        ti = b // per_shard
+        k0 = (b % per_shard) * per_block
+        feats = pl.ds(pl.multiple_of(t * depth, depth), depth)
+        lhs = rows[ti // 2, pl.ds(k0, per_block), ti % 2, :, feats].reshape(BLOCK, depth)
+        part[b] = jnp.dot(lhs, rdown[which], preferred_element_type=jnp.float32)
+        return carry
+
+    lax.fori_loop(0, n_block, shrink, 0)
+
+    mine = pl.ds(c * half, half)
+    others = pl.ds(oc * half, half)
+    e0 = remote_copy(part.at[others], rs1, es_sem.at[0], er_sem.at[0], sibling)
+    e0.start()
+    e0.wait()
+    mid[...] = part[mine] + rs1[...]
+    e1 = remote_copy(mid, rs2, es_sem.at[1], er_sem.at[1], peer)
+    e1.start()
+    e1.wait()
+    sh[mine] = (mid[...] + rs2[...]).astype(jnp.bfloat16)
+    e2 = remote_copy(sh.at[mine], sh.at[mine], es_sem.at[2], er_sem.at[2], sibling)
+    e2.start()
+    e2.wait()
+
+    def finish(b, carry):
+        which, place = layout(b)
+        at = pl.ds(pl.multiple_of(b * BLOCK, BLOCK), BLOCK)
+        low = sh[b]
+        dk = jnp.dot(low[:, :ADAPTER_RANK], rup[which, 0], preferred_element_type=jnp.float32)
+        dv = jnp.dot(low[:, ADAPTER_RANK:], rup[which, 1], preferred_element_type=jnp.float32)
+        vals_out[at, :] = (accv[at, :] + adapter_scale * dv).astype(jnp.bfloat16)
+        p = acck[at, :] + adapter_scale * dk
+        cos, sin = cos_ref[place], sin_ref[place]
+        for h in range(p.shape[1] // HD):
+            head = p[:, h * HD : (h + 1) * HD]
+            turned = head * cos + pltpu.roll(head, HD // 2, 1) * sin
+            keys_out[at, h * HD : (h + 1) * HD] = turned.astype(jnp.bfloat16)
+        return carry
+
+    lax.fori_loop(0, n_block, finish, 0)
+
+
+def rotary_tables(blocks):
+    frequency = np.float32(rope_base) ** (
+        np.float32(-2.0) * np.arange(HD // 2, dtype=np.float32) / np.float32(HD)
+    )
+    angles = np.arange(blocks * BLOCK, dtype=np.float32)[:, None] * frequency[None, :]
+    wide = angles.astype(np.float64)
+    cos = np.concatenate([np.cos(wide), np.cos(wide)], axis=1).astype(np.float32)
+    sin = np.concatenate([-np.sin(wide), np.sin(wide)], axis=1).astype(np.float32)
+    return cos.reshape(blocks, BLOCK, HD), sin.reshape(blocks, BLOCK, HD)
+
+
+def fused(
+    n_store,
+    tokens,
+    attention_norm_gain,
+    key_weight,
+    value_weight,
+    adapter_down_weight,
+    adapter_up_weight,
+    storage_slot_adapter,
+    request_adapter,
+    segment_blocks,
+):
+    shard, width = tokens.shape
+    cols = key_weight.shape[1]
+    total = 4 * shard
+    n_chunk = shard // CHUNK
+    n_block = total // BLOCK
+    seg_count = segment_blocks.shape[1]
+    stored, depth, ranks = adapter_down_weight.shape
+    up_shape = adapter_up_weight.shape[1:]
+    cos, sin = rotary_tables(n_block - seg_count + 1)
+    bf16, f32 = jnp.bfloat16, jnp.float32
+    any_spec = pl.BlockSpec(memory_space=pl.ANY)
+    vmem = pl.BlockSpec(memory_space=pltpu.VMEM)
+    smem = pl.BlockSpec(memory_space=pltpu.SMEM)
+    dma = pltpu.SemaphoreType.DMA
+    half = n_block // 2
+    return pl.pallas_call(
+        functools.partial(fused_kernel, n_store),
+        out_shape=[jax.ShapeDtypeStruct((total, cols), bf16)] * 2,
+        in_specs=[any_spec, vmem, any_spec, any_spec, any_spec, any_spec, smem, smem, smem, vmem, vmem],
+        out_specs=[vmem, vmem],
+        scratch_shapes=[
+            pltpu.VMEM((shard, width), bf16),
+            pltpu.VMEM((2, n_chunk, 2, CHUNK, width), bf16),
+            pltpu.VMEM((width, cols), bf16),
+            pltpu.VMEM((width, cols), bf16),
+            pltpu.VMEM((stored, depth, ranks), bf16),
+            pltpu.VMEM((stored,) + up_shape, bf16),
+            pltpu.VMEM((seg_count, depth, ranks), bf16),
+            pltpu.VMEM((seg_count,) + up_shape, bf16),
+            pltpu.VMEM((seg_count, depth, ranks), bf16),
+            pltpu.VMEM((seg_count,) + up_shape, bf16),
+            pltpu.VMEM((total, cols), f32),
+            pltpu.VMEM((total, cols), f32),
+            pltpu.VMEM((n_block, BLOCK, ranks), f32),
+            pltpu.VMEM((half, BLOCK, ranks), f32),
+            pltpu.VMEM((half, BLOCK, ranks), f32),
+            pltpu.VMEM((half, BLOCK, ranks), f32),
+            pltpu.VMEM((n_block, BLOCK, ranks), bf16),
+            dma((n_chunk,)), dma((4,)), dma((n_chunk,)), dma((n_chunk,)), dma((n_chunk,)),
+            dma((n_chunk,)), dma((n_chunk,)), dma((n_chunk,)),
+            dma((seg_count,)), dma((seg_count,)), dma((seg_count,)), dma((seg_count,)),
+            dma((3,)), dma((3,)),
+        ],
+        compiler_params=pltpu.CompilerParams(
+            collective_id=0, has_side_effects=True, vmem_limit_bytes=56 * 1024 * 1024
+        ),
+        cost_estimate=pl.CostEstimate(
+            flops=2 * total * (2 * width * cols + depth * ranks),
+            bytes_accessed=2 * (shard * width + 2 * width * cols + 2 * total * cols),
+            transcendentals=0,
+        ),
+    )(
+        tokens,
+        attention_norm_gain.reshape(1, width),
+        key_weight,
+        value_weight,
+        adapter_down_weight,
+        adapter_up_weight,
+        storage_slot_adapter,
+        request_adapter,
+        segment_blocks,
+        jnp.asarray(cos),
+        jnp.asarray(sin),
+    )
+
+
 def solution(mesh):
     in_specs = (
         P(("parts", "store", "tensor"), None),
@@ -125,6 +451,9 @@
         P(("parts", "store"), None),
     )
     out_specs = (P(("parts", "store"), ("tensor", "sub")), P(("parts", "store"), ("tensor", "sub")))
+    body = per_device
+    if mesh.shape["sub"] == 1 and mesh.shape["tensor"] == 4:
+        body = functools.partial(fused, mesh.shape["store"])
     return jax.shard_map(
-        per_device, mesh=mesh, in_specs=in_specs, out_specs=out_specs, check_vma=False
-    )
+        body, mesh=mesh, in_specs=in_specs, out_specs=out_specs, check_vma=False
+    )

time: 392 us -> 122 us (0.31)
  waiting for transfers between devices: 313 us -> 0 us
  Pallas kernels: 0 us -> 118 us
  matrix products: 23.4 us -> 0 us
  blocking collectives: 16.3 us -> 0 us
  between operations: 13.9 us -> 0.64 us
  local copies, waits for them, and re-layouts: 15.7 us -> 3.74 us
  other arithmetic: 9.25 us -> 0 us
    all_gather x3 -> x0, waiting for transfers between devices: 312 us -> none  [the longest x1 175 us: per_device(): lax.all_gather(adapter_down_weight, 'store', axis=0, tiled=True)]
    pallas_call x0 -> x1, Pallas kernels: none -> 118 us  [fused(): pl.pallas_call(functools.partial(fused_kernel, n_store), out_shape=[jax.S...]
    dot_general x4 -> x0, matrix products: 23.4 us -> none  [the longest x1 12.2 us: per_device(): jnp.dot(piece, value_weight, preferred_element_type=jnp.float32)]
    psum x1 -> x0, blocking collectives: 16.3 us -> none  [per_device(): shrunk = lax.psum(partial_sum, ('tensor', 'sub')).astype(jnp.bfloat16)]
    gather x2 -> x0, local copies, waits for them, and re-layouts: 9.77 us -> none  [the longest x1 7.79 us: per_device(): block_down = down_table[block_slot]]
  transfers between devices with their start and end apart: 3 -> 0, of which waited for: 3 -> 0; matrix products, arithmetic and copies ran while one was open for 5% -> 0% of each run, Pallas kernels for 0% -> 0%
where the time goes in v1:
time: 122 us
  Pallas kernels  118 us (97%)
  local copies, waits for them, and re-layouts  3.74 us (3%)
    pallas_call x1, Pallas kernels, fused(): pl.pallas_call(functools.partial(fused_kernel, n_store), out_shape=[jax.S...  118 us
    unnamed x2, local copies, waits for them, and re-layouts  3.74 us

profile of v1, /device:TPU:0, one launch (start us, length us, event | category | flops | bytes accessed | tf_op | source)
XLA Modules:
  0.0 122.1 jit_solution(1895878414225812557)
XLA Ops:
  0.6 117.7 %shard_map.122 = (bf16[1024,256]{1,0:T(8,128)(2,1)}, bf16[1024,256]{1,0:T(8,128)(2,1)}) custom-call(bf16[256,8192]{1,0:T(8,128)(2,1)} %tok_hbm.1, f32[1,8192]{1,0:T(1,128)} %bitcast.1, bf16[8192,256]{1,0:T(8,128)(2,1)} %kw_hbm.1, bf16[8192,256]{1,0:T(8,128)(2,1)} %vw_hbm.1, bf16[3,2048,128]{2,1,0:T(8,128)(2,1)} %down_hbm.1, bf16[3,2,64,256]{3,2,1,0:T(8,128)(2,1)} %up_hbm.1, ...), custom_call_target="tpu_custom_call" | custom-call | flops 9126805504 | bytes 13631488 | tf_op jit(solution)/shard_map/pallas_call | solution.py:390
  118.3 1.9 %copy.15 = bf16[1024,256]{1,0:T(8,128)(2,1)} copy(bf16[1024,256]{1,0:T(8,128)(2,1)} %get-tuple-element.4) | data formatting | bytes 1048576
  120.2 1.9 %copy.16 = bf16[1024,256]{1,0:T(8,128)(2,1)} copy(bf16[1024,256]{1,0:T(8,128)(2,1)} %get-tuple-element.5) | data formatting | bytes 1048576

commit v2 on v1

--- a/solution.py
+++ b/solution.py
@@ -122,19 +122,18 @@
 
 def fused_kernel(
     n_store,
-    tok_hbm, gain, kw_hbm, vw_hbm, down_hbm, up_hbm, slots, req, seg, cos_ref, sin_ref,
+    tok_hbm, gain, kw_hbm, vw_hbm, down_hbm, up_hbm, slots, req, seg, cos_hbm, sin_hbm,
     keys_out, vals_out,
-    tok, rows, kw, vw, down, up, sdown, sup, rdown, rup, acck, accv, part, rs1, mid, rs2, sh,
-    tok_sem, w_sem, xs_sem, xr_sem, ss_sem, sr_sem, fs_sem, fr_sem,
-    ds_sem, dr_sem, us_sem, ur_sem, es_sem, er_sem,
+    tok, rows, kw, vw, down, up, sdown, sup, rdown, rup, acck, accv, cos_ref, sin_ref, *rest_refs,
 ):
+    early, late = rest_refs[:6], rest_refs[6:12]
+    (tok_sem, w_sem, xs_sem, xr_sem, ss_sem, sr_sem, fs_sem, fr_sem,
+     ds_sem, dr_sem, us_sem, ur_sem, es_sem, er_sem) = rest_refs[12:]
     n_chunk = rows.shape[1]
     shard = n_chunk * CHUNK
     seg_count = rdown.shape[0]
     stored = down.shape[0]
     depth = down.shape[1]
-    n_block = part.shape[0]
-    half = n_block // 2
     store = lax.axis_index("store")
     t = lax.axis_index("tensor")
     x, c = t // 2, t % 2
@@ -150,6 +149,13 @@
     def src_of(j):
         return lax.rem(store + offsets[j], n_store)
 
+    barrier = pltpu.get_barrier_semaphore()
+    greet = [peer, sibling]
+    for j in remote:
+        greet += [{"store": dst_of(j)}, {"store": src_of(j)}]
+    for who in greet:
+        pl.semaphore_signal(barrier, inc=1, device_id=who, device_id_type=pl.DeviceIdType.MESH)
+
     def tok_copy(k):
         r = pl.ds(pl.multiple_of(k * CHUNK, CHUNK), CHUNK)
         return pltpu.make_async_copy(tok_hbm.at[r], tok.at[r], tok_sem.at[k])
@@ -159,21 +165,16 @@
         pltpu.make_async_copy(up_hbm, up, w_sem.at[1]),
         pltpu.make_async_copy(kw_hbm, kw, w_sem.at[2]),
         pltpu.make_async_copy(vw_hbm, vw, w_sem.at[3]),
+        pltpu.make_async_copy(cos_hbm, cos_ref, w_sem.at[4]),
+        pltpu.make_async_copy(sin_hbm, sin_ref, w_sem.at[5]),
     ]
     tok_copy(0).start()
     loads[0].start()
     loads[1].start()
     for k in range(1, n_chunk):
         tok_copy(k).start()
-    loads[2].start()
-    loads[3].start()
-
-    barrier = pltpu.get_barrier_semaphore()
-    greet = [peer, sibling]
-    for j in remote:
-        greet += [{"store": dst_of(j)}, {"store": src_of(j)}]
-    for who in greet:
-        pl.semaphore_signal(barrier, inc=1, device_id=who, device_id_type=pl.DeviceIdType.MESH)
+    for load in loads[2:]:
+        load.start()
 
     def remote_copy(src, dst, ssem, rsem, who):
         return pltpu.make_async_remote_copy(
@@ -226,7 +227,6 @@
             sdown[j] = down[local]
             sup[j] = up[local]
             d_copy(j).start()
-            u_copy(j).start()
         else:
             rdown[j] = down[local]
             rup[j] = up[local]
@@ -270,15 +270,7 @@
 
     lax.fori_loop(0, n_chunk // group, sibling_rows, 0)
 
-    def far_rows(k, carry):
-        x_copy(k).wait()
-        f_copy(k).start()
-
-        @pl.when(k + 2 < n_chunk)
-        def _():
-            x_copy(k + 2).start()
-
-        f_copy(k).wait()
+    def project_far(k):
         lhs = rows[ox, k].reshape(2 * CHUNK, kw.shape[0])
         pk = jnp.dot(lhs, kw[...], preferred_element_type=jnp.float32)
         pv = jnp.dot(lhs, vw[...], preferred_element_type=jnp.float32)
@@ -286,13 +278,23 @@
             at = pl.ds(pl.multiple_of((ox * 2 + ci) * shard + k * CHUNK, CHUNK), CHUNK)
             acck[at, :] = pk[ci * CHUNK : (ci + 1) * CHUNK]
             accv[at, :] = pv[ci * CHUNK : (ci + 1) * CHUNK]
+
+    def far_rows(k, carry):
+        x_copy(k).wait()
+        f_copy(k).start()
+
+        @pl.when(k + 2 < n_chunk)
+        def _():
+            x_copy(k + 2).start()
+
+        f_copy(k).wait()
+        project_far(k)
         return carry
 
-    lax.fori_loop(0, n_chunk, far_rows, 0)
-
+    lax.fori_loop(0, n_chunk - 2, far_rows, 0)
     for j in remote:
-        d_copy(j).wait()
-        u_copy(j).wait()
+        u_copy(j).start()
+    lax.fori_loop(n_chunk - 2, n_chunk - 1, far_rows, 0)
 
     def layout(b):
         end, which, first = jnp.int32(0), jnp.int32(0), jnp.int32(0)
@@ -305,48 +307,104 @@
 
     per_block = BLOCK // CHUNK
     per_shard = shard // BLOCK
-
-    def shrink(b, carry):
-        which, _ = layout(b)
-        ti = b // per_shard
-        k0 = (b % per_shard) * per_block
-        feats = pl.ds(pl.multiple_of(t * depth, depth), depth)
-        lhs = rows[ti // 2, pl.ds(k0, per_block), ti % 2, :, feats].reshape(BLOCK, depth)
-        part[b] = jnp.dot(lhs, rdown[which], preferred_element_type=jnp.float32)
-        return carry
-
-    lax.fori_loop(0, n_block, shrink, 0)
-
-    mine = pl.ds(c * half, half)
-    others = pl.ds(oc * half, half)
-    e0 = remote_copy(part.at[others], rs1, es_sem.at[0], er_sem.at[0], sibling)
-    e0.start()
-    e0.wait()
-    mid[...] = part[mine] + rs1[...]
-    e1 = remote_copy(mid, rs2, es_sem.at[1], er_sem.at[1], peer)
-    e1.start()
-    e1.wait()
-    sh[mine] = (mid[...] + rs2[...]).astype(jnp.bfloat16)
-    e2 = remote_copy(sh.at[mine], sh.at[mine], es_sem.at[2], er_sem.at[2], sibling)
-    e2.start()
-    e2.wait()
-
-    def finish(b, carry):
-        which, place = layout(b)
-        at = pl.ds(pl.multiple_of(b * BLOCK, BLOCK), BLOCK)
-        low = sh[b]
-        dk = jnp.dot(low[:, :ADAPTER_RANK], rup[which, 0], preferred_element_type=jnp.float32)
-        dv = jnp.dot(low[:, ADAPTER_RANK:], rup[which, 1], preferred_element_type=jnp.float32)
-        vals_out[at, :] = (accv[at, :] + adapter_scale * dv).astype(jnp.bfloat16)
-        p = acck[at, :] + adapter_scale * dk
-        cos, sin = cos_ref[place], sin_ref[place]
-        for h in range(p.shape[1] // HD):
-            head = p[:, h * HD : (h + 1) * HD]
-            turned = head * cos + pltpu.roll(head, HD // 2, 1) * sin
-            keys_out[at, h * HD : (h + 1) * HD] = turned.astype(jnp.bfloat16)
-        return carry
-
-    lax.fori_loop(0, n_block, finish, 0)
+    feats = pl.ds(pl.multiple_of(t * depth, depth), depth)
+    first_pieces = [(i, i * per_block, per_block) for i in range(per_shard)]
+    first_pieces[-1] = (per_shard - 1, (per_shard - 1) * per_block, per_block - 1)
+    last_pieces = [(per_shard - 1, n_chunk - 1, 1)]
+
+    def shrink(pieces, part):
+        base = pieces[0][1]
+
+        def source(ti, carry):
+            for i, k0, count in pieces:
+                which, _ = layout(ti * per_shard + i)
+                lhs = rows[ti // 2, k0 : k0 + count, ti % 2, :, feats].reshape(count * CHUNK, depth)
+                part[ti, (k0 - base) * CHUNK : (k0 - base + count) * CHUNK, :] = jnp.dot(
+                    lhs, rdown[which], preferred_element_type=jnp.float32
+                )
+            return carry
+
+        lax.fori_loop(0, 4, source, 0)
+
+    def finish(pieces, sh):
+        base = pieces[0][1]
+
+        def source(ti, carry):
+            for i, k0, count in pieces:
+                n = count * CHUNK
+                which, place = layout(ti * per_shard + i)
+                at = pl.ds(pl.multiple_of(ti * shard + k0 * CHUNK, CHUNK), n)
+                start = (k0 - i * per_block) * CHUNK
+                low = sh[ti, (k0 - base) * CHUNK : (k0 - base) * CHUNK + n, :]
+                dk = jnp.dot(
+                    low[:, :ADAPTER_RANK], rup[which, 0], preferred_element_type=jnp.float32
+                )
+                dv = jnp.dot(
+                    low[:, ADAPTER_RANK:], rup[which, 1], preferred_element_type=jnp.float32
+                )
+                vals_out[at, :] = (accv[at, :] + adapter_scale * dv).astype(jnp.bfloat16)
+                p = acck[at, :] + adapter_scale * dk
+                cos = cos_ref[place, start : start + n, :]
+                sin = sin_ref[place, start : start + n, :]
+                for h in range(p.shape[1] // HD):
+                    head = p[:, h * HD : (h + 1) * HD]
+                    turned = head * cos + pltpu.roll(head, HD // 2, 1) * sin
+                    keys_out[at, h * HD : (h + 1) * HD] = turned.astype(jnp.bfloat16)
+            return carry
+
+        lax.fori_loop(0, 4, source, 0)
+
+    mine = pl.ds(c * 2, 2)
+    others = pl.ds(oc * 2, 2)
+
+    def pair_copy(bufs, n):
+        return remote_copy(bufs[0].at[others], bufs[1], es_sem.at[n], er_sem.at[n], sibling)
+
+    def cross_copy(bufs, n):
+        return remote_copy(bufs[3], bufs[4], es_sem.at[n], er_sem.at[n], peer)
+
+    def share_copy(bufs, n):
+        return remote_copy(bufs[5].at[mine], bufs[5].at[mine], es_sem.at[n], er_sem.at[n], sibling)
+
+    def add_pair(bufs):
+        part, rs1, mid, narrow, _, _ = bufs
+        mid[...] = part[mine] + rs1[...]
+        narrow[...] = mid[...].astype(jnp.bfloat16)
+
+    def add_cross(bufs):
+        _, _, mid, _, rs2, sh = bufs
+        sh[mine] = (mid[...] + rs2[...].astype(jnp.float32)).astype(jnp.bfloat16)
+
+    for j in remote:
+        d_copy(j).wait()
+    shrink(first_pieces, early[0])
+    pair_copy(early, 0).start()
+    pair_copy(early, 0).wait()
+    add_pair(early)
+    cross_copy(early, 1).start()
+    x_copy(n_chunk - 1).wait()
+    f_copy(n_chunk - 1).start()
+    cross_copy(early, 1).wait()
+    add_cross(early)
+    share_copy(early, 2).start()
+    f_copy(n_chunk - 1).wait()
+    shrink(last_pieces, late[0])
+    pair_copy(late, 3).start()
+    project_far(n_chunk - 1)
+    pair_copy(late, 3).wait()
+    add_pair(late)
+    cross_copy(late, 4).start()
+    share_copy(early, 2).wait()
+    for j in remote:
+        u_copy(j).wait()
+    loads[4].wait()
+    loads[5].wait()
+    finish(first_pieces, early[5])
+    cross_copy(late, 4).wait()
+    add_cross(late)
+    share_copy(late, 5).start()
+    share_copy(late, 5).wait()
+    finish(last_pieces, late[5])
 
 
 def rotary_tables(blocks):
@@ -386,11 +444,21 @@
     vmem = pl.BlockSpec(memory_space=pltpu.VMEM)
     smem = pl.BlockSpec(memory_space=pltpu.SMEM)
     dma = pltpu.SemaphoreType.DMA
-    half = n_block // 2
-    return pl.pallas_call(
+    def exchange(n):
+        return [
+            pltpu.VMEM((4, n, ranks), f32),
+            pltpu.VMEM((2, n, ranks), f32),
+            pltpu.VMEM((2, n, ranks), f32),
+            pltpu.VMEM((2, n, ranks), bf16),
+            pltpu.VMEM((2, n, ranks), bf16),
+            pltpu.VMEM((4, n, ranks), bf16),
+        ]
+
+    outs = [jax.ShapeDtypeStruct((total, cols), bf16)] * 2
+    made = pl.pallas_call(
         functools.partial(fused_kernel, n_store),
-        out_shape=[jax.ShapeDtypeStruct((total, cols), bf16)] * 2,
-        in_specs=[any_spec, vmem, any_spec, any_spec, any_spec, any_spec, smem, smem, smem, vmem, vmem],
+        out_shape=outs,
+        in_specs=[any_spec, vmem, any_spec, any_spec, any_spec, any_spec, smem, smem, smem, any_spec, any_spec],
         out_specs=[vmem, vmem],
         scratch_shapes=[
             pltpu.VMEM((shard, width), bf16),
@@ -405,15 +473,14 @@
             pltpu.VMEM((seg_count,) + up_shape, bf16),
             pltpu.VMEM((total, cols), f32),
             pltpu.VMEM((total, cols), f32),
-            pltpu.VMEM((n_block, BLOCK, ranks), f32),
-            pltpu.VMEM((half, BLOCK, ranks), f32),
-            pltpu.VMEM((half, BLOCK, ranks), f32),
-            pltpu.VMEM((half, BLOCK, ranks), f32),
-            pltpu.VMEM((n_block, BLOCK, ranks), bf16),
-            dma((n_chunk,)), dma((4,)), dma((n_chunk,)), dma((n_chunk,)), dma((n_chunk,)),
+            pltpu.VMEM(cos.shape, f32),
+            pltpu.VMEM(sin.shape, f32),
+            *exchange(shard - CHUNK),
+            *exchange(CHUNK),
+            dma((n_chunk,)), dma((6,)), dma((n_chunk,)), dma((n_chunk,)), dma((n_chunk,)),
             dma((n_chunk,)), dma((n_chunk,)), dma((n_chunk,)),
             dma((seg_count,)), dma((seg_count,)), dma((seg_count,)), dma((seg_count,)),
-            dma((3,)), dma((3,)),
+            dma((6,)), dma((6,)),
         ],
         compiler_params=pltpu.CompilerParams(
             collective_id=0, has_side_effects=True, vmem_limit_bytes=56 * 1024 * 1024
@@ -436,6 +503,7 @@
         jnp.asarray(cos),
         jnp.asarray(sin),
     )
+    return made
 
 
 def solution(mesh):

time: 122 us -> 114 us (0.934)
  Pallas kernels: 118 us -> 110 us
    pallas_call x1, Pallas kernels: 118 us -> 110 us  [fused(): pl.pallas_call(functools.partial(fused_kernel, n_store), out_shape=outs,...]
where the time goes in v2:
time: 114 us
  Pallas kernels  110 us (96%)
  local copies, waits for them, and re-layouts  3.74 us (3%)
    pallas_call x1, Pallas kernels, fused(): pl.pallas_call(functools.partial(fused_kernel, n_store), out_shape=outs,...  110 us
    unnamed x2, local copies, waits for them, and re-layouts  3.74 us

profile of v2, /device:TPU:0, one launch (start us, length us, event | category | flops | bytes accessed | tf_op | source)
XLA Modules:
  0.0 113.9 jit_solution(10785420364821091552)
XLA Ops:
  0.6 109.5 %shard_map.122 = (bf16[1024,256]{1,0:T(8,128)(2,1)}, bf16[1024,256]{1,0:T(8,128)(2,1)}) custom-call(bf16[256,8192]{1,0:T(8,128)(2,1)} %tok_hbm.1, f32[1,8192]{1,0:T(1,128)} %bitcast.1, bf16[8192,256]{1,0:T(8,128)(2,1)} %kw_hbm.1, bf16[8192,256]{1,0:T(8,128)(2,1)} %vw_hbm.1, bf16[3,2048,128]{2,1,0:T(8,128)(2,1)} %down_hbm.1, bf16[3,2,64,256]{3,2,1,0:T(8,128)(2,1)} %up_hbm.1, ...), custom_call_target="tpu_custom_call" | custom-call | flops 9126805504 | bytes 13631488 | tf_op jit(solution)/shard_map/pallas_call | solution.py:458
  110.2 1.9 %copy.15 = bf16[1024,256]{1,0:T(8,128)(2,1)} copy(bf16[1024,256]{1,0:T(8,128)(2,1)} %get-tuple-element.4) | data formatting | bytes 1048576
  112.0 1.9 %copy.16 = bf16[1024,256]{1,0:T(8,128)(2,1)} copy(bf16[1024,256]{1,0:T(8,128)(2,1)} %get-tuple-element.5) | data formatting | bytes 1048576

commit v3 on v2

--- a/solution.py
+++ b/solution.py
@@ -294,7 +294,9 @@
     lax.fori_loop(0, n_chunk - 2, far_rows, 0)
     for j in remote:
         u_copy(j).start()
-    lax.fori_loop(n_chunk - 2, n_chunk - 1, far_rows, 0)
+    x_copy(n_chunk - 2).wait()
+    f_copy(n_chunk - 2).start()
+    f_copy(n_chunk - 2).wait()
 
     def layout(b):
         end, which, first = jnp.int32(0), jnp.int32(0), jnp.int32(0)
@@ -312,10 +314,11 @@
     first_pieces[-1] = (per_shard - 1, (per_shard - 1) * per_block, per_block - 1)
     last_pieces = [(per_shard - 1, n_chunk - 1, 1)]
 
-    def shrink(pieces, part):
+    def shrink(pieces, part, first, number):
         base = pieces[0][1]
 
-        def source(ti, carry):
+        def source(i_source, carry):
+            ti = first + i_source
             for i, k0, count in pieces:
                 which, _ = layout(ti * per_shard + i)
                 lhs = rows[ti // 2, k0 : k0 + count, ti % 2, :, feats].reshape(count * CHUNK, depth)
@@ -324,7 +327,7 @@
                 )
             return carry
 
-        lax.fori_loop(0, 4, source, 0)
+        lax.fori_loop(0, number, source, 0)
 
     def finish(pieces, sh):
         base = pieces[0][1]
@@ -377,18 +380,21 @@
 
     for j in remote:
         d_copy(j).wait()
-    shrink(first_pieces, early[0])
+    shrink(first_pieces, early[0], 0, 4)
     pair_copy(early, 0).start()
+    shrink(last_pieces, late[0], x * 2, 2)
     pair_copy(early, 0).wait()
     add_pair(early)
     cross_copy(early, 1).start()
+    project_far(n_chunk - 2)
     x_copy(n_chunk - 1).wait()
     f_copy(n_chunk - 1).start()
+    shrink(last_pieces, late[0], ox * 2 + c, 1)
     cross_copy(early, 1).wait()
     add_cross(early)
     share_copy(early, 2).start()
     f_copy(n_chunk - 1).wait()
-    shrink(last_pieces, late[0])
+    shrink(last_pieces, late[0], ox * 2 + oc, 1)
     pair_copy(late, 3).start()
     project_far(n_chunk - 1)
     pair_copy(late, 3).wait()
@@ -405,6 +411,11 @@
     share_copy(late, 5).start()
     share_copy(late, 5).wait()
     finish(last_pieces, late[5])
+
+
+def copy_kernel(a, b, c, d):
+    c[...] = a[...]
+    d[...] = b[...]
 
 
 def rotary_tables(blocks):
@@ -503,7 +514,14 @@
         jnp.asarray(cos),
         jnp.asarray(sin),
     )
-    return made
+    block = pl.BlockSpec((total // 2, cols), lambda i: (i, 0))
+    return pl.pallas_call(
+        copy_kernel,
+        grid=(2,),
+        out_shape=outs,
+        in_specs=[block, block],
+        out_specs=[block, block],
+    )(*made)
 
 
 def solution(mesh):

time: 114 us -> 112 us (0.982)
  local copies, waits for them, and re-layouts: 3.74 us -> 0 us
    unnamed x2 -> x0, local copies, waits for them, and re-layouts: 3.74 us -> none
    pallas_call x0 -> x1, Pallas kernels: none -> 2.04 us  [fused(): pl.pallas_call(copy_kernel, grid=(2,), out_shape=outs, in_specs=[block, b...]
where the time goes in v3:
time: 112 us
  Pallas kernels  111 us (99%)
    pallas_call x1, Pallas kernels, fused(): pl.pallas_call(functools.partial(fused_kernel, n_store), out_shape=outs,...  109 us

profile of v3, /device:TPU:0, one launch (start us, length us, event | category | flops | bytes accessed | tf_op | source)
XLA Modules:
  0.0 111.6 jit_solution(11794601365949313175)
XLA Ops:
  0.6 108.9 %shard_map.122 = (bf16[1024,256]{1,0:T(8,128)(2,1)}, bf16[1024,256]{1,0:T(8,128)(2,1)}) custom-call(bf16[256,8192]{1,0:T(8,128)(2,1)} %tok_hbm.1, f32[1,8192]{1,0:T(1,128)} %bitcast.1, bf16[8192,256]{1,0:T(8,128)(2,1)} %kw_hbm.1, bf16[8192,256]{1,0:T(8,128)(2,1)} %vw_hbm.1, bf16[3,2048,128]{2,1,0:T(8,128)(2,1)} %down_hbm.1, bf16[3,2,64,256]{3,2,1,0:T(8,128)(2,1)} %up_hbm.1, ...), custom_call_target="tpu_custom_call" | custom-call | flops 9126805504 | bytes 13631488 | tf_op jit(solution)/shard_map/pallas_call | solution.py:469
  109.5 2.0 %shard_map.123 = (bf16[1024,256]{1,0:T(8,128)(2,1)}, bf16[1024,256]{1,0:T(8,128)(2,1)}) custom-call(bf16[1024,256]{1,0:T(8,128)(2,1)} %get-tuple-element.4.a, bf16[1024,256]{1,0:T(8,128)(2,1)} %get-tuple-element.5.b), custom_call_target="tpu_custom_call" | custom-call | tf_op jit(solution)/shard_map/pallas_call | solution.py:518
